TPU v7x, 128 devices: a whole 4x4x4 slice. The times are simulated.
128 devices in a mesh: row: 4 (over z_hi, core), tm: 32 (over y, z_lo, x).
Axes of the slice: x: 4, y: 4, z: 4 (z_hi: 2, z_lo: 2; z = z_hi * 2 + z_lo), core: 2. Of those that a mesh axis runs over, the one named last changes fastest.
Arguments:
- temps: bfloat16 [24576, 16384], P('row', 'tm')
- area: float32 [24576], P('row'), may hold values from 0.2 to 1
- ocean_rows: int32 [24576], P('row'), may hold values from 0 to 6143, as said below
- counts: int32 [4], P('row'), may hold values from 1536 to 6144, as said below
Outputs:
- band: float32 [2048, 16384], P('row', 'tm')
Inputs may be any that keep to these rules, and one draw needn't show every extreme that they name: `ocean_rows`: within each tile of 6144 entries, every local row number appears once. `counts`: some tile is all ocean.
All inputs are finite; a program needn't handle non-finite values.
Results may differ from a plain program's by a relative error of at most 0.0022.
Values may be sent and summed in bfloat16 or wider, within the bound.
A program may use at most 64 MiB of HBM per device.

v0:
```python
import jax
import jax.numpy as jnp
from jax import lax
from jax.sharding import PartitionSpec as P

LAGS = 4


def shifted(value, axis, steps):
    count = lax.axis_size(axis)
    pairs = [(source, (source + steps) % count) for source in range(count)]
    return lax.ppermute(value, axis, pairs)


def body(temps, area, ocean_rows, counts):
    rows, hours = temps.shape
    total_hours = hours * lax.axis_size("tm")
    total_rows = rows * lax.axis_size("row")
    sums = jnp.sum(temps, axis=1, dtype=jnp.float32)
    mean = lax.psum(sums, "tm") / total_hours
    live = (jnp.arange(rows, dtype=jnp.int32) < counts[0]).astype(jnp.float32)
    ocean = jnp.zeros((rows,), jnp.float32).at[ocean_rows].set(live)
    weighted = ((temps.astype(jnp.float32) - mean[:, None]) * (ocean * area)[:, None]).astype(
        jnp.bfloat16
    )
    others = [weighted]
    current = weighted
    for lag in range(1, LAGS):
        current = shifted(current, "tm", -1)
        others.append(current)
    joined = jnp.concatenate(others, axis=1)
    contract = (((0,), (0,)), ((), ()))
    terms = lax.dot_general(joined, weighted, contract, preferred_element_type=jnp.float32)
    summed = lax.psum_scatter(terms, "row", scatter_dimension=0, tiled=True)
    return summed / jnp.sqrt(jnp.float32(total_rows))


def solution(mesh):
    in_specs = (P("row", "tm"), P("row"), P("row"), P("row"))
    out_specs = P("row", "tm")
    return jax.shard_map(body, mesh=mesh, in_specs=in_specs, out_specs=out_specs, check_vma=False)
```

profile of v0, /device:TPU:71, one launch (start us, length us, event | category | flops | bytes accessed | tf_op | source)
XLA Modules:
  0.0 651.7 jit_solution(8619647536048842335)
XLA Ops:
  6.5 0.0 copy-start
  6.5 0.0 reduce-scatter.2.cloned.1.call-start
  7.2 0.7 compare_select_fusion
  8.0 3.7 convert_reduce_fusion
  11.7 119.8 %psum.7 = f32[6144]{0:T(1024)S(1)} all-reduce(f32[6144]{0:T(1024)S(1)} %convert_reduce_fusion), channel_id=1, replica_groups=mesh['row'=4,'tm'=32] {'tm'}, use_global_device_ids=true, to_apply=%region_1.0 | all-reduce | flops 6144 | bytes 49152 | tf_op jit(solution)/shard_map/psum | solution.py:20
  131.4 23.0 %scatter_custom_fusion = f32[6144]{0:T(1024)S(1)} fusion(s32[6144]{0:T(1024)S(1)} %compare_select_fusion, f32[6144]{0:T(1024)S(1)} %fusion.10, f32[]{:T(128)} %constant.5.clone.1), kind=kCustom, calls=%fused_computation.17 | custom fusion | bytes 24580 | tf_op jit(solution)/shard_map/scatter | solution.py:22
  154.4 0.0 copy-done
  154.5 4.4 fusion.9
  158.9 6.0 collective-permute-start
  165.0 106.2 %collective-permute-done = bf16[6144,512]{1,0:T(8,128)(2,1)S(1)} collective-permute-done((bf16[6144,512]{1,0:T(8,128)(2,1)S(1)}, bf16[6144,512]{1,0:T(8,128)(2,1)S(1)}, u32[]{:S(2)}, u32[]{:S(2)}) %collective-permute-start) | collective-permute-done | bytes 6291488 | tf_op jit(solution)/shard_map/ppermute | solution.py:12
  271.1 2.2 collective-permute-start.1
  273.3 131.8 %collective-permute-done.1 = bf16[6144,512]{1,0:T(8,128)(2,1)S(1)} collective-permute-done((bf16[6144,512]{1,0:T(8,128)(2,1)S(1)}, bf16[6144,512]{1,0:T(8,128)(2,1)S(1)}, u32[]{:S(2)}, u32[]{:S(2)}) %collective-permute-start.1) | collective-permute-done | bytes 6291488 | tf_op jit(solution)/shard_map/ppermute | solution.py:12
  405.1 2.2 collective-permute-start.2
  407.3 131.8 %collective-permute-done.2 = bf16[6144,512]{1,0:T(8,128)(2,1)} collective-permute-done((bf16[6144,512]{1,0:T(8,128)(2,1)S(1)}, bf16[6144,512]{1,0:T(8,128)(2,1)}, u32[]{:S(2)}, u32[]{:S(2)}) %collective-permute-start.2) | collective-permute-done | bytes 6291488 | tf_op jit(solution)/shard_map/ppermute | solution.py:12
  539.1 17.6 %fusion = f32[2048,512]{1,0:T(8,128)} fusion(bf16[6144,512]{1,0:T(8,128)(2,1)S(1)} %fusion.9, bf16[6144,512]{1,0:T(8,128)(2,1)} %collective-permute-done.2, bf16[6144,512]{1,0:T(8,128)(2,1)S(1)} %collective-permute-done.1, bf16[6144,512]{1,0:T(8,128)(2,1)S(1)} %collective-permute-done), kind=kOutput, calls=%fused_computation.1 | convolution fusion | flops 12985565184 | bytes 29360128 | tf_op jit(solution)/shard_map/dot_general | solution.py:33
  556.7 0.0 reduce-scatter.2.cloned.1.call-update
  556.7 85.8 %reduce-scatter.2.cloned.1.call-done = f32[512,512]{1,0:T(8,128)} async-done(((f32[2048,512]{1,0:T(8,128)}), f32[512,512]{1,0:T(8,128)}) %reduce-scatter.2.cloned.1.call-update) | async-done | bytes 1048592 | tf_op jit(solution)/shard_map/reduce_scatter | solution.py:34
  642.6 2.3 broadcast_multiply_fusion
  (3 shorter events, 0.0 us)
Async XLA Ops:
  6.5 147.9 %copy-start = (f32[6144]{0:T(1024)S(1)}, f32[6144]{0:T(1024)}, u32[]{:S(2)}) copy-start(f32[6144]{0:T(1024)} %param.5) | copy-start | bytes 73732
  6.5 636.0 %reduce-scatter.2.cloned.1.call-start = ((), (), s32[]{:S(2)}) async-start(), calls=%async_computation.1 | async-start | bytes 5242880 | tf_op jit(solution)/shard_map/reduce_scatter | solution.py:34
  158.9 112.2 %collective-permute-start = (bf16[6144,512]{1,0:T(8,128)(2,1)S(1)}, bf16[6144,512]{1,0:T(8,128)(2,1)S(1)}, u32[]{:S(2)}, u32[]{:S(2)}) collective-permute-start(bf16[6144,512]{1,0:T(8,128)(2,1)S(1)} %fusion.9), channel_id=1, source_target_pairs={{0,31},{1,0},{2,1},{3,2},{4,3},{5,4},{6,5},{7,6},{8,7},{9,8},{10,9... | collective-permute-start | bytes 18874376 | tf_op jit(solution)/shard_map/ppermute | solution.py:12
  271.1 134.0 %collective-permute-start.1 = (bf16[6144,512]{1,0:T(8,128)(2,1)S(1)}, bf16[6144,512]{1,0:T(8,128)(2,1)S(1)}, u32[]{:S(2)}, u32[]{:S(2)}) collective-permute-start(bf16[6144,512]{1,0:T(8,128)(2,1)S(1)} %collective-permute-done), channel_id=1, source_target_pairs={{0,31},{1,0},{2,1},{3,2},{4,3},{5,4},{6,5},{7,6},{8,7},{9,8},{10,9... | collective-permute-start | bytes 18874376 | tf_op jit(solution)/shard_map/ppermute | solution.py:12
  405.1 134.0 %collective-permute-start.2 = (bf16[6144,512]{1,0:T(8,128)(2,1)S(1)}, bf16[6144,512]{1,0:T(8,128)(2,1)}, u32[]{:S(2)}, u32[]{:S(2)}) collective-permute-start(bf16[6144,512]{1,0:T(8,128)(2,1)S(1)} %collective-permute-done.1), channel_id=1, source_target_pairs={{0,31},{1,0},{2,1},{3,2},{4,3},{5,4},{6,5},{7,6},{8,7},{9,8},{10,9... | collective-permute-start | bytes 18874376 | tf_op jit(solution)/shard_map/ppermute | solution.py:12
Sparse Core Ops, SparseCore 0:
  556.8 85.6 reduce-scatter.1
where the time goes:
time: 656 us; the launch traced here: 652 us
  waiting for transfers between devices  456 us (70%)
  blocking collectives  120 us (18%)
  local copies, waits for them, and re-layouts  23 us (4%)
  matrix products  17.6 us (3%)
  between operations  14.1 us (2%)
  other arithmetic  11.2 us (2%)
  starting transfers between devices  10.4 us (2%)
    ppermute x3, waiting for transfers between devices, shifted(): return lax.ppermute(value, axis, pairs)  370 us
    psum x1, blocking collectives, body(): mean = lax.psum(sums, 'tm') / total_hours  120 us
    reduce_scatter x1, waiting for transfers between devices, body(): summed = lax.psum_scatter(terms, 'row', scatter_dimension=0, tiled=True)  85.8 us
    scatter x1, local copies, waits for them, and re-layouts, body(): ocean = jnp.zeros((rows,), jnp.float32).at[ocean_rows].set(live)  23 us
    dot_general x1, matrix products, body(): lax.dot_general(joined, weighted, contract, preferred_element_type=jnp.fl...  17.6 us
  transfers between devices with their start and end apart: 4, of which 4 were waited for; matrix products, arithmetic and copies ran while one was open for 0% of the time, Pallas kernels for 0%

commit v1 on v0

v1 whole, which is shorter than its diff:
```python
import functools
import math

import jax
import jax.numpy as jnp
from jax import lax
from jax.experimental import pallas as pl
from jax.experimental.pallas import tpu as pltpu
from jax.sharding import PartitionSpec as P

LAGS = 4
NX = 4
NG = 8
LANES = 128
CHUNK = 256
EARLY = 3
MESH = pl.DeviceIdType.MESH
F32 = jnp.float32
BF16 = jnp.bfloat16
CROSS_ROWS = (((0,), (0,)), ((), ()))
CROSS_LANES = (((1,), (1,)), ((), ()))
PAIRS = (
    [(i, k) for i in range(NX) for k in range(LAGS) if i + k < NX],
    [(1, 3), (2, 2), (3, 1)],
    [(2, 3), (3, 2)],
    [(3, 3)],
)


def kernel(
    temps, area, listed, count, out,
    raw, halo, weighted, own, csend, crecv, xsend, xrecv, zsend, zrecv,
    sums, near, partial, far, means, scales, local_sem,
    xs_sem, xr_sem, hs_sem, hr_sem, cs_sem, cr_sem, ps_sem, pr_sem, zs_sem, zr_sem,
    ns_sem, nr_sem, fs_sem, fr_sem,
):
    row, tm = lax.axis_index("row"), lax.axis_index("tm")
    zh, core = row // 2, lax.rem(row, 2)
    group, x = tm // NX, lax.rem(tm, NX)
    quarter = raw.shape[1]
    chunks = quarter // CHUNK
    tiles = quarter // LANES
    hours = raw.shape[2]

    def x_peer(step):
        return (row, group * NX + lax.rem(x + step, NX))

    def g_peer(step):
        return (row, lax.rem(group + step, NG) * NX + x)

    partner = (zh * 2 + 1 - core, tm)
    opposite = (lax.rem(row + 2, 4), tm)
    x_at = [lax.rem(x + step, NX) for step in range(NX)]

    barrier = pltpu.get_barrier_semaphore()
    everyone = [x_peer(s) for s in range(1, NX)] + [g_peer(s) for s in range(1, NG)]
    everyone += [partner, opposite]
    for device in everyone:
        pl.semaphore_signal(barrier, inc=1, device_id=device, device_id_type=MESH)

    def remote(src, dst, send, recv, device):
        return pltpu.make_async_remote_copy(
            src_ref=src, dst_ref=dst, send_sem=send, recv_sem=recv, device_id=device, device_id_type=MESH
        )

    def rows_of(piece, base=0):
        return pl.ds(pl.multiple_of(base + piece * CHUNK, CHUNK), CHUNK)

    stage = [
        pltpu.make_async_copy(
            temps.at[pl.ds(q * quarter, quarter)], weighted.at[q], local_sem.at[q]
        )
        for q in range(NX)
    ]
    keep = pltpu.make_async_copy(
        temps.at[pl.ds(pl.multiple_of(x * quarter, quarter), quarter)], raw.at[x], local_sem.at[NX]
    )
    for copy in stage:
        copy.start()
    keep.start()

    def exchange(step, piece):
        target = x_at[step]
        return remote(
            temps.at[rows_of(piece, target * quarter)], raw.at[x, rows_of(piece)],
            xs_sem.at[step - 1, piece], xr_sem.at[NX - step - 1, piece], x_peer(step),
        )

    def arrival(step, piece):
        source = x_at[step]
        return remote(
            temps.at[rows_of(piece)], raw.at[source, rows_of(piece)],
            xs_sem.at[0, 0], xr_sem.at[step - 1, piece], x_peer(step),
        )

    def forward(block, piece):
        return remote(
            raw.at[block, rows_of(piece)], halo.at[block, rows_of(piece)],
            hs_sem.at[block, piece], hr_sem.at[block, piece], g_peer(NG - 1),
        )

    def forward_own(piece):
        return remote(
            temps.at[rows_of(piece, x * quarter)], halo.at[x, rows_of(piece)],
            hs_sem.at[x, piece], hr_sem.at[x, piece], g_peer(NG - 1),
        )

    pl.semaphore_wait(barrier, len(everyone))

    for piece in range(chunks):
        exchange(1, piece).start()
        exchange(3, piece).start()
    for piece in range(chunks):
        @pl.when((x < 2) | ((x == 2) & (piece < EARLY)))
        def _():
            forward_own(piece).start()
    for piece in range(chunks):
        exchange(2, piece).start()

    sums[...] = jnp.zeros_like(sums)
    ones = jnp.ones((8, hours), BF16)
    for q in range(NX):
        stage[q].wait()
        for piece in range(quarter // 512):
            some = lax.dot_general(
                ones, weighted[q, pl.ds(piece * 512, 512)], CROSS_LANES, preferred_element_type=F32
            )
            for part in range(4):
                sums[q, pl.ds(piece * 4 + part, 1)] = some[0:1, part * LANES : (part + 1) * LANES]
    keep.wait()

    def send_near(step):
        return remote(
            sums.at[x_at[step]], near.at[NX - step - 1], ns_sem.at[step - 1], nr_sem.at[NX - step - 1], x_peer(step)
        )

    def send_far(step):
        return remote(partial, far.at[NG - step - 1], fs_sem.at[step - 1], fr_sem.at[NG - step - 1], g_peer(step))

    for step in range(1, NX):
        send_near(step).start()

    per = listed.shape[1]
    live = count[0]
    mask = jnp.zeros((16, LANES), F32)
    for part in range(listed.shape[0]):
        value = listed[pl.ds(part, 1), :]
        high = jnp.broadcast_to(value // LANES - x * tiles, (16, per))
        low = jnp.broadcast_to(value % LANES, (LANES, per))
        place = lax.broadcasted_iota(jnp.int32, (LANES, per), 1) + part * per
        left = jnp.where(high == lax.broadcasted_iota(jnp.int32, (16, per), 0), 1.0, 0.0).astype(BF16)
        hit = (low == lax.broadcasted_iota(jnp.int32, (LANES, per), 0)) & (place < live)
        right = jnp.where(hit, 1.0, 0.0).astype(BF16)
        mask = mask + lax.dot_general(left, right, CROSS_LANES, preferred_element_type=F32)
    scale = mask[:tiles] * area[x]

    def spread(row_values, target):
        for a in range(tiles):
            target[pl.ds(a * LANES, LANES)] = jnp.broadcast_to(row_values[a : a + 1], (LANES, LANES)).T

    spread(scale, scales)

    def pass_on(step, piece):
        arrival(step, piece).wait_recv()
        @pl.when(x_at[step] < NX - 1)
        def _():
            forward(x_at[step], piece).start()

    for piece in range(2):
        pass_on(3, piece)
        pass_on(1, piece)

    for step in range(1, NX):
        send_near(step).wait_recv()
    partial[...] = sums[x] + near[0] + near[1] + near[2]
    for step in range(1, NG):
        send_far(step).start()

    for piece in range(2, chunks):
        pass_on(3, piece)
        pass_on(1, piece)

    for step in range(1, NG):
        send_far(step).wait_recv()
    total = partial[...]
    for step in range(NG - 1):
        total = total + far[step]
    spread(total[:tiles] / (hours * NX * NG), means)

    def weigh(source, target, piece):
        r = rows_of(piece)
        m, s = means[r], scales[r]
        for lane in range(0, hours, LANES):
            at = pl.ds(lane, LANES)
            target[r, at] = ((source[r, at].astype(F32) - m) * s).astype(BF16)

    for piece in range(chunks):
        pass_on(2, piece)
        for step in (0, 1, 3):
            weigh(raw.at[x_at[step]], weighted.at[x_at[step]], piece)
        weigh(raw.at[x_at[2]], weighted.at[x_at[2]], piece)
    for piece in range(EARLY, chunks):
        @pl.when(x == 2)
        def _():
            forward_own(piece).start()

    def slot_of(i, k):
        return i * 2 + k // 2

    def swap(slot):
        return remote(csend.at[slot], crecv.at[slot], cs_sem.at[slot], cr_sem.at[slot], partner)

    def to_owner(i, k):
        away = lax.rem(x - i + NX, NX)
        at = lax.rem(away + NX - 1, NX)
        return remote(
            xsend.at[slot_of(i, k)], xrecv.at[at, k // 2],
            ps_sem.at[slot_of(i, k)], pr_sem.at[at, k // 2], (row, group * NX + i),
        )

    def multiply(i, k):
        value = lax.dot_general(weighted[i + k], weighted[i], CROSS_ROWS, preferred_element_type=F32)
        slot = slot_of(i, k)
        mine = core == k % 2

        @pl.when(mine)
        def _():
            own[slot] = value

        @pl.when(jnp.logical_not(mine))
        def _():
            csend[slot] = value
            swap(slot).start()

    def finish(i, k):
        slot = slot_of(i, k)

        @pl.when(core == k % 2)
        def _():
            swap(slot).wait_recv()

            @pl.when(x == i)
            def _():
                own[slot] = own[slot] + crecv[slot]

            @pl.when(x != i)
            def _():
                xsend[slot] = (own[slot] + crecv[slot]).astype(BF16)
                to_owner(i, k).start()

    waiting = []
    for stage_at, pairs in enumerate(PAIRS):
        if stage_at:
            block = stage_at - 1
            for piece in range(chunks):
                forward(block, piece).wait_recv()
                weigh(halo.at[block], weighted.at[NX + block], piece)
        for pair in pairs:
            multiply(*pair)
            waiting.append(pair)
            if len(waiting) > 2:
                finish(*waiting.pop(0))
    for pair in waiting:
        finish(*pair)

    def gathered(kk):
        for d in range(NX - 1):
            remote(
                xsend.at[0], xrecv.at[d, kk], ps_sem.at[0], pr_sem.at[d, kk], x_peer(d + 1)
            ).wait_recv()
        value = own[x * 2 + kk]
        for d in range(NX - 1):
            value = value + xrecv[d, kk].astype(F32)
        return value

    across = remote(zsend, zrecv, zs_sem, zr_sem, opposite)
    zsend[...] = gathered(1 - zh).astype(BF16)
    across.start()
    mine = gathered(zh)
    across.wait_recv()
    out[...] = (mine + zrecv[...].astype(F32)) / math.sqrt(quarter * NX * 4)

    for step in range(1, NX):
        for piece in range(chunks):
            exchange(step, piece).wait_send()
        send_near(step).wait_send()
    for step in range(1, NG):
        send_far(step).wait_send()
    for block in range(NX - 1):
        for piece in range(chunks):
            forward(block, piece).wait_send()
    for i in range(NX):
        for k in range(LAGS):
            slot = slot_of(i, k)

            @pl.when(core != k % 2)
            def _():
                swap(slot).wait_send()

            @pl.when((core == k % 2) & (x != i))
            def _():
                to_owner(i, k).wait_send()
    across.wait_send()


def body(temps, area, ocean_rows, counts):
    rows, hours = temps.shape
    quarter = rows // NX
    chunks = quarter // CHUNK
    vmem = pl.BlockSpec(memory_space=pltpu.VMEM)
    dma = pltpu.SemaphoreType.DMA
    return pl.pallas_call(
        kernel,
        out_shape=jax.ShapeDtypeStruct((hours, hours), F32),
        in_specs=[
            pl.BlockSpec(memory_space=pl.ANY), vmem, vmem, pl.BlockSpec(memory_space=pltpu.SMEM),
        ],
        out_specs=vmem,
        scratch_shapes=[
            pltpu.VMEM((NX, quarter, hours), BF16),
            pltpu.VMEM((NX - 1, quarter, hours), BF16),
            pltpu.VMEM((2 * NX - 1, quarter, hours), BF16),
            pltpu.VMEM((2 * NX, hours, hours), F32),
            pltpu.VMEM((2 * NX, hours, hours), F32),
            pltpu.VMEM((2 * NX, hours, hours), F32),
            pltpu.VMEM((2 * NX, hours, hours), BF16),
            pltpu.VMEM((NX - 1, 2, hours, hours), BF16),
            pltpu.VMEM((hours, hours), BF16),
            pltpu.VMEM((hours, hours), BF16),
            pltpu.VMEM((NX, 16, LANES), F32),
            pltpu.VMEM((NX - 1, 16, LANES), F32),
            pltpu.VMEM((16, LANES), F32),
            pltpu.VMEM((NG - 1, 16, LANES), F32),
            pltpu.VMEM((quarter, LANES), F32),
            pltpu.VMEM((quarter, LANES), F32),
            dma((NX + 1,)),
            dma((NX - 1, chunks)), dma((NX - 1, chunks)),
            dma((NX - 1, chunks)), dma((NX - 1, chunks)),
            dma((2 * NX,)), dma((2 * NX,)),
            dma((2 * NX,)), dma((NX - 1, 2)),
            dma, dma,
            dma((NX - 1,)), dma((NX - 1,)),
            dma((NG - 1,)), dma((NG - 1,)),
        ],
        compiler_params=pltpu.CompilerParams(
            collective_id=0, has_side_effects=True, vmem_limit_bytes=62 << 20
        ),
        cost_estimate=pl.CostEstimate(
            flops=2 * LAGS * hours * hours * rows, bytes_accessed=2 * rows * hours, transcendentals=0
        ),
        name="lagged_band",
    )(temps, area.reshape(NX, -1, LANES), ocean_rows.reshape(8, -1), counts)


def solution(mesh):
    in_specs = (P("row", "tm"), P("row"), P("row"), P("row"))
    out_specs = P("row", "tm")
    return jax.shard_map(body, mesh=mesh, in_specs=in_specs, out_specs=out_specs, check_vma=False)
```

time: 656 us -> 190 us (0.29)
  the two profiles are of different devices: /device:TPU:71 before, /device:TPU:101 now
where the time goes in v1:
time: 190 us; the launch traced here: 189 us
  Pallas kernels  184 us (97%)
  local copies, waits for them, and re-layouts  4.96 us (3%)
    pallas_call x1, Pallas kernels, body(): pl.pallas_call(kernel, out_shape=jax.ShapeDtypeStruct((hours, hours), F32...  184 us

profile of v1, /device:TPU:101, one launch (start us, length us, event | category | flops | bytes accessed | tf_op | source)
XLA Modules:
  0.0 189.3 jit_solution(13456354780765515790)
XLA Ops:
  0.7 1.3 reshape.7.listed
  2.0 1.4 reshape.6.area
  3.3 183.7 %lagged_band.1 = f32[512,512]{1,0:T(8,128)} custom-call(bf16[6144,512]{1,0:T(8,128)(2,1)} %temps.1, f32[4,12,128]{2,1,0:T(8,128)} %reshape.6.area, s32[8,768]{1,0:T(8,128)} %reshape.7.listed, s32[1]{0:T(128)S(6)} %copy.6.count), custom_call_target="tpu_custom_call" | custom-call | flops 12884901888 | bytes 6291456 | tf_op jit(solution)/shard_map/lagged_band/pallas_call | solution.py:312
  187.1 2.3 %copy.7 = f32[512,512]{1,0:T(8,128)} copy(f32[512,512]{1,0:T(8,128)} %lagged_band.1) | data formatting | bytes 2097152

commit v2 on v1

--- a/solution.py
+++ b/solution.py
@@ -13,7 +13,8 @@
 NG = 8
 LANES = 128
 CHUNK = 256
-EARLY = 3
+EARLY = 2
+WINDOW = 3
 MESH = pl.DeviceIdType.MESH
 F32 = jnp.float32
 BF16 = jnp.bfloat16
@@ -30,7 +31,7 @@
 def kernel(
     temps, area, listed, count, out,
     raw, halo, weighted, own, csend, crecv, xsend, xrecv, zsend, zrecv,
-    sums, near, partial, far, means, scales, local_sem,
+    sums, near, partial, far, scale, means, scales, local_sem,
     xs_sem, xr_sem, hs_sem, hr_sem, cs_sem, cr_sem, ps_sem, pr_sem, zs_sem, zr_sem,
     ns_sem, nr_sem, fs_sem, fr_sem,
 ):
@@ -107,15 +108,13 @@
 
     pl.semaphore_wait(barrier, len(everyone))
 
-    for piece in range(chunks):
+    for piece in range(WINDOW):
         exchange(1, piece).start()
         exchange(3, piece).start()
     for piece in range(chunks):
-        @pl.when((x < 2) | ((x == 2) & (piece < EARLY)))
+        @pl.when((x == 0) | ((x < NX - 1) & (piece < EARLY)))
         def _():
             forward_own(piece).start()
-    for piece in range(chunks):
-        exchange(2, piece).start()
 
     sums[...] = jnp.zeros_like(sums)
     ones = jnp.ones((8, hours), BF16)
@@ -140,36 +139,55 @@
     for step in range(1, NX):
         send_near(step).start()
 
-    per = listed.shape[1]
+    def one_hop(piece):
+        arrival(3, piece).wait_recv()
+        arrival(1, piece).wait_recv()
+
+        @pl.when((x == 1) | (x == 2))
+        def _():
+            forward(x - 1, piece).start()
+
+        @pl.when(x == 3)
+        def _():
+            forward(0, piece).start()
+
+        if piece < EARLY:
+            @pl.when(x == 3)
+            def _():
+                forward(2, piece).start()
+        if piece + WINDOW < chunks:
+            exchange(1, piece + WINDOW).start()
+            exchange(3, piece + WINDOW).start()
+        else:
+            some = chunks // WINDOW
+            for late in range(some):
+                exchange(2, (piece + WINDOW - chunks) * some + late).start()
+
+    one_hop(0)
+
     live = count[0]
-    mask = jnp.zeros((16, LANES), F32)
-    for part in range(listed.shape[0]):
+    groups = listed.shape[0]
+
+    def mark(part, mask):
         value = listed[pl.ds(part, 1), :]
-        high = jnp.broadcast_to(value // LANES - x * tiles, (16, per))
-        low = jnp.broadcast_to(value % LANES, (LANES, per))
-        place = lax.broadcasted_iota(jnp.int32, (LANES, per), 1) + part * per
-        left = jnp.where(high == lax.broadcasted_iota(jnp.int32, (16, per), 0), 1.0, 0.0).astype(BF16)
-        hit = (low == lax.broadcasted_iota(jnp.int32, (LANES, per), 0)) & (place < live)
+        high = jnp.broadcast_to(value // LANES, (groups, LANES))
+        low = jnp.broadcast_to(value % LANES, (LANES, LANES))
+        place = lax.broadcasted_iota(jnp.int32, (LANES, LANES), 1) + part * LANES
+        left = jnp.where(high == lax.broadcasted_iota(jnp.int32, (groups, LANES), 0), 1.0, 0.0).astype(BF16)
+        hit = (low == lax.broadcasted_iota(jnp.int32, (LANES, LANES), 0)) & (place < live)
         right = jnp.where(hit, 1.0, 0.0).astype(BF16)
-        mask = mask + lax.dot_general(left, right, CROSS_LANES, preferred_element_type=F32)
-    scale = mask[:tiles] * area[x]
-
-    def spread(row_values, target):
+        return mask + lax.dot_general(left, right, CROSS_LANES, preferred_element_type=F32)
+
+    mask = lax.fori_loop(0, groups, mark, jnp.zeros((groups, LANES), F32))
+    scale[...] = mask * area[...]
+
+    def spread(row_of, target):
         for a in range(tiles):
-            target[pl.ds(a * LANES, LANES)] = jnp.broadcast_to(row_values[a : a + 1], (LANES, LANES)).T
-
-    spread(scale, scales)
-
-    def pass_on(step, piece):
-        arrival(step, piece).wait_recv()
-        @pl.when(x_at[step] < NX - 1)
-        def _():
-            forward(x_at[step], piece).start()
-
-    for piece in range(2):
-        pass_on(3, piece)
-        pass_on(1, piece)
-
+            target[pl.ds(a * LANES, LANES)] = jnp.broadcast_to(row_of(a), (LANES, LANES)).T
+
+    spread(lambda a: scale[pl.ds(x * tiles + a, 1)], scales)
+
+    one_hop(1)
     for step in range(1, NX):
         send_near(step).wait_recv()
     partial[...] = sums[x] + near[0] + near[1] + near[2]
@@ -177,15 +195,24 @@
         send_far(step).start()
 
     for piece in range(2, chunks):
-        pass_on(3, piece)
-        pass_on(1, piece)
+        one_hop(piece)
+
+    for piece in range(chunks):
+        @pl.when(x == 0)
+        def _():
+            forward(1, piece).start()
+        if piece >= EARLY:
+            @pl.when(x == 1)
+            def _():
+                forward_own(piece).start()
 
     for step in range(1, NG):
         send_far(step).wait_recv()
     total = partial[...]
     for step in range(NG - 1):
         total = total + far[step]
-    spread(total[:tiles] / (hours * NX * NG), means)
+    mean = total[:tiles] / (hours * NX * NG)
+    spread(lambda a: mean[a : a + 1], means)
 
     def weigh(source, target, piece):
         r = rows_of(piece)
@@ -195,14 +222,26 @@
             target[r, at] = ((source[r, at].astype(F32) - m) * s).astype(BF16)
 
     for piece in range(chunks):
-        pass_on(2, piece)
         for step in (0, 1, 3):
             weigh(raw.at[x_at[step]], weighted.at[x_at[step]], piece)
+        arrival(2, piece).wait_recv()
+
+        @pl.when(x != 1)
+        def _():
+            forward(x_at[2], piece).start()
         weigh(raw.at[x_at[2]], weighted.at[x_at[2]], piece)
-    for piece in range(EARLY, chunks):
-        @pl.when(x == 2)
-        def _():
-            forward_own(piece).start()
+    for piece in range(chunks):
+        @pl.when(x == 1)
+        def _():
+            forward(2, piece).start()
+        if piece >= EARLY:
+            @pl.when(x == 2)
+            def _():
+                forward_own(piece).start()
+
+            @pl.when(x == 3)
+            def _():
+                forward(2, piece).start()
 
     def slot_of(i, k):
         return i * 2 + k // 2
@@ -260,8 +299,8 @@
             waiting.append(pair)
             if len(waiting) > 2:
                 finish(*waiting.pop(0))
-    for pair in waiting:
-        finish(*pair)
+        while waiting:
+            finish(*waiting.pop(0))
 
     def gathered(kk):
         for d in range(NX - 1):
@@ -331,6 +370,7 @@
             pltpu.VMEM((NX - 1, 16, LANES), F32),
             pltpu.VMEM((16, LANES), F32),
             pltpu.VMEM((NG - 1, 16, LANES), F32),
+            pltpu.VMEM((rows // LANES, LANES), F32),
             pltpu.VMEM((quarter, LANES), F32),
             pltpu.VMEM((quarter, LANES), F32),
             dma((NX + 1,)),
@@ -349,7 +389,7 @@
             flops=2 * LAGS * hours * hours * rows, bytes_accessed=2 * rows * hours, transcendentals=0
         ),
         name="lagged_band",
-    )(temps, area.reshape(NX, -1, LANES), ocean_rows.reshape(8, -1), counts)
+    )(temps, area.reshape(-1, LANES), ocean_rows.reshape(-1, LANES), counts)
 
 
 def solution(mesh):

time: 190 us -> 155 us (0.82)
  the two profiles are of different devices: /device:TPU:101 before, /device:TPU:71 now
where the time goes in v2:
time: 155 us
  Pallas kernels  152 us (98%)
  local copies, waits for them, and re-layouts  2.26 us (1%)
    pallas_call x1, Pallas kernels, body(): pl.pallas_call(kernel, out_shape=jax.ShapeDtypeStruct((hours, hours), F32...  152 us

profile of v2, /device:TPU:71, one launch (start us, length us, event | category | flops | bytes accessed | tf_op | source)
XLA Modules:
  0.0 155.0 jit_solution(11507156405572012912)
XLA Ops:
  0.7 152.1 %lagged_band.1 = f32[512,512]{1,0:T(8,128)} custom-call(bf16[6144,512]{1,0:T(8,128)(2,1)} %temps.1, f32[48,128]{1,0:T(8,128)} %bitcast.2, s32[48,128]{1,0:T(8,128)} %bitcast.3, s32[1]{0:T(128)S(6)} %copy.6.count), custom_call_target="tpu_custom_call" | custom-call | flops 12884901888 | bytes 6291456 | tf_op jit(solution)/shard_map/lagged_band/pallas_call | solution.py:351
  152.8 2.3 %copy.7 = f32[512,512]{1,0:T(8,128)} copy(f32[512,512]{1,0:T(8,128)} %lagged_band.1) | data formatting | bytes 2097152

commit v3 on v2

--- a/solution.py
+++ b/solution.py
@@ -20,12 +20,18 @@
 BF16 = jnp.bfloat16
 CROSS_ROWS = (((0,), (0,)), ((), ()))
 CROSS_LANES = (((1,), (1,)), ((), ()))
-PAIRS = (
-    [(i, k) for i in range(NX) for k in range(LAGS) if i + k < NX],
-    [(1, 3), (2, 2), (3, 1)],
-    [(2, 3), (3, 2)],
-    [(3, 3)],
-)
+PARTS = 2
+
+
+def without(x, with_far):
+    far = (x + 2) % NX
+    pairs = [(i, k) for k in range(LAGS) for i in range(NX) if i + k < NX]
+    return [(i, k) for i, k in pairs if (far in (i, i + k)) == with_far]
+
+
+EARLY_PAIRS = list(zip(*[without(x, False) for x in range(NX)]))
+LATE_PAIRS = list(zip(*[without(x, True) for x in range(NX)]))
+CROSS_PAIRS = [[(1, 3), (2, 2), (3, 1)], [(2, 3), (3, 2)], [(3, 3)]]
 
 
 def kernel(
@@ -42,6 +48,7 @@
     chunks = quarter // CHUNK
     tiles = quarter // LANES
     hours = raw.shape[2]
+    half = hours // PARTS
 
     def x_peer(step):
         return (row, group * NX + lax.rem(x + step, NX))
@@ -221,15 +228,85 @@
             at = pl.ds(lane, LANES)
             target[r, at] = ((source[r, at].astype(F32) - m) * s).astype(BF16)
 
+    def pick(values):
+        value = values[0]
+        for at in range(1, NX):
+            value = jnp.where(x == at, values[at], value)
+        return value
+
+    def lag_pair(pairs):
+        return pick([i for i, _ in pairs]), pick([k for _, k in pairs])
+
+    def slot_of(i, k):
+        return i * 2 + k // 2
+
+    def part_of(part):
+        return pl.ds(part * half, half)
+
+    def swap(slot, part):
+        return remote(
+            csend.at[slot, part_of(part)], crecv.at[slot, part_of(part)],
+            cs_sem.at[slot, part], cr_sem.at[slot, part], partner,
+        )
+
+    def to_owner(i, k, part):
+        away = lax.rem(x - i + NX, NX)
+        at = lax.rem(away + NX - 1, NX)
+        slot = slot_of(i, k)
+        return remote(
+            xsend.at[slot, part_of(part)], xrecv.at[at, k // 2, part_of(part)],
+            ps_sem.at[slot, part], pr_sem.at[at, k // 2, part], (row, group * NX + i),
+        )
+
+    def multiply(i, k):
+        slot = slot_of(i, k)
+        mine = core == lax.rem(k, 2)
+        for part in range(PARTS):
+            value = lax.dot_general(
+                weighted[i + k, :, part * half : (part + 1) * half], weighted[i],
+                CROSS_ROWS, preferred_element_type=F32,
+            )
+
+            @pl.when(mine)
+            def _():
+                own[slot, part_of(part)] = value
+
+            @pl.when(jnp.logical_not(mine))
+            def _():
+                csend[slot, part_of(part)] = value
+                swap(slot, part).start()
+
+    def finish(i, k):
+        slot = slot_of(i, k)
+
+        @pl.when(core == lax.rem(k, 2))
+        def _():
+            for part in range(PARTS):
+                at = part_of(part)
+                swap(slot, part).wait_recv()
+
+                @pl.when(x == i)
+                def _():
+                    own[slot, at] = own[slot, at] + crecv[slot, at]
+
+                @pl.when(x != i)
+                def _():
+                    xsend[slot, at] = (own[slot, at] + crecv[slot, at]).astype(BF16)
+                    to_owner(i, k, part).start()
+
     for piece in range(chunks):
         for step in (0, 1, 3):
             weigh(raw.at[x_at[step]], weighted.at[x_at[step]], piece)
+    early = [lag_pair(pairs) for pairs in EARLY_PAIRS]
+    for piece in range(chunks):
         arrival(2, piece).wait_recv()
 
         @pl.when(x != 1)
         def _():
             forward(x_at[2], piece).start()
         weigh(raw.at[x_at[2]], weighted.at[x_at[2]], piece)
+        if piece < len(early):
+            multiply(*early[piece])
     for piece in range(chunks):
         @pl.when(x == 1)
         def _():
@@ -243,52 +320,9 @@
             def _():
                 forward(2, piece).start()
 
-    def slot_of(i, k):
-        return i * 2 + k // 2
-
-    def swap(slot):
-        return remote(csend.at[slot], crecv.at[slot], cs_sem.at[slot], cr_sem.at[slot], partner)
-
-    def to_owner(i, k):
-        away = lax.rem(x - i + NX, NX)
-        at = lax.rem(away + NX - 1, NX)
-        return remote(
-            xsend.at[slot_of(i, k)], xrecv.at[at, k // 2],
-            ps_sem.at[slot_of(i, k)], pr_sem.at[at, k // 2], (row, group * NX + i),
-        )
-
-    def multiply(i, k):
-        value = lax.dot_general(weighted[i + k], weighted[i], CROSS_ROWS, preferred_element_type=F32)
-        slot = slot_of(i, k)
-        mine = core == k % 2
-
-        @pl.when(mine)
-        def _():
-            own[slot] = value
-
-        @pl.when(jnp.logical_not(mine))
-        def _():
-            csend[slot] = value
-            swap(slot).start()
-
-    def finish(i, k):
-        slot = slot_of(i, k)
-
-        @pl.when(core == k % 2)
-        def _():
-            swap(slot).wait_recv()
-
-            @pl.when(x == i)
-            def _():
-                own[slot] = own[slot] + crecv[slot]
-
-            @pl.when(x != i)
-            def _():
-                xsend[slot] = (own[slot] + crecv[slot]).astype(BF16)
-                to_owner(i, k).start()
-
-    waiting = []
-    for stage_at, pairs in enumerate(PAIRS):
+    waiting = early
+    stages = [[lag_pair(pairs) for pairs in LATE_PAIRS]] + CROSS_PAIRS
+    for stage_at, pairs in enumerate(stages):
         if stage_at:
             block = stage_at - 1
             for piece in range(chunks):
@@ -297,27 +331,48 @@
         for pair in pairs:
             multiply(*pair)
             waiting.append(pair)
-            if len(waiting) > 2:
+            while len(waiting) > 2:
                 finish(*waiting.pop(0))
-        while waiting:
-            finish(*waiting.pop(0))
-
-    def gathered(kk):
+        if stage_at < len(stages) - 1:
+            while waiting:
+                finish(*waiting.pop(0))
+
+    def gathered(kk, part):
         for d in range(NX - 1):
             remote(
-                xsend.at[0], xrecv.at[d, kk], ps_sem.at[0], pr_sem.at[d, kk], x_peer(d + 1)
+                xsend.at[0, part_of(part)], xrecv.at[d, kk, part_of(part)],
+                ps_sem.at[0, part], pr_sem.at[d, kk, part], x_peer(d + 1),
             ).wait_recv()
-        value = own[x * 2 + kk]
+        value = own[x * 2 + kk, part_of(part)]
         for d in range(NX - 1):
-            value = value + xrecv[d, kk].astype(F32)
+            value = value + xrecv[d, kk, part_of(part)].astype(F32)
         return value
 
-    across = remote(zsend, zrecv, zs_sem, zr_sem, opposite)
-    zsend[...] = gathered(1 - zh).astype(BF16)
-    across.start()
-    mine = gathered(zh)
-    across.wait_recv()
-    out[...] = (mine + zrecv[...].astype(F32)) / math.sqrt(quarter * NX * 4)
+    def across(part):
+        return remote(
+            zsend.at[part_of(part)], zrecv.at[part_of(part)], zs_sem.at[part], zr_sem.at[part], opposite
+        )
+
+    def send_across():
+        for part in range(PARTS):
+            zsend[part_of(part)] = gathered(1 - zh, part).astype(BF16)
+            across(part).start()
+
+    last = (x == NX - 1) & (core == 1) & (zh == 0)
+
+    @pl.when(jnp.logical_not(last))
+    def _():
+        send_across()
+    while waiting:
+        finish(*waiting.pop(0))
+
+    @pl.when(last)
+    def _():
+        send_across()
+    for part in range(PARTS):
+        value = gathered(zh, part)
+        across(part).wait_recv()
+        out[part_of(part)] = (value + zrecv[part_of(part)].astype(F32)) / math.sqrt(quarter * NX * 4)
 
     for step in range(1, NX):
         for piece in range(chunks):
@@ -330,16 +385,16 @@
             forward(block, piece).wait_send()
     for i in range(NX):
         for k in range(LAGS):
-            slot = slot_of(i, k)
-
-            @pl.when(core != k % 2)
-            def _():
-                swap(slot).wait_send()
-
-            @pl.when((core == k % 2) & (x != i))
-            def _():
-                to_owner(i, k).wait_send()
-    across.wait_send()
+            for part in range(PARTS):
+                @pl.when(core != k % 2)
+                def _():
+                    swap(slot_of(i, k), part).wait_send()
+
+                @pl.when((core == k % 2) & (x != i))
+                def _():
+                    to_owner(i, k, part).wait_send()
+    for part in range(PARTS):
+        across(part).wait_send()
 
 
 def body(temps, area, ocean_rows, counts):
@@ -376,9 +431,9 @@
             dma((NX + 1,)),
             dma((NX - 1, chunks)), dma((NX - 1, chunks)),
             dma((NX - 1, chunks)), dma((NX - 1, chunks)),
-            dma((2 * NX,)), dma((2 * NX,)),
-            dma((2 * NX,)), dma((NX - 1, 2)),
-            dma, dma,
+            dma((2 * NX, PARTS)), dma((2 * NX, PARTS)),
+            dma((2 * NX, PARTS)), dma((NX - 1, 2, PARTS)),
+            dma((PARTS,)), dma((PARTS,)),
             dma((NX - 1,)), dma((NX - 1,)),
             dma((NG - 1,)), dma((NG - 1,)),
         ],

time: 155 us -> 143 us (0.923)
  Pallas kernels: 152 us -> 140 us
    pallas_call x1, Pallas kernels: 152 us -> 140 us  [body(): pl.pallas_call(kernel, out_shape=jax.ShapeDtypeStruct((hours, hours), F32...]
where the time goes in v3:
time: 143 us
  Pallas kernels  140 us (98%)
  local copies, waits for them, and re-layouts  2.26 us (2%)
    pallas_call x1, Pallas kernels, body(): pl.pallas_call(kernel, out_shape=jax.ShapeDtypeStruct((hours, hours), F32...  140 us

profile of v3, /device:TPU:71, one launch (start us, length us, event | category | flops | bytes accessed | tf_op | source)
XLA Modules:
  0.0 142.8 jit_solution(5920943479992722370)
XLA Ops:
  0.7 139.8 %lagged_band.1 = f32[512,512]{1,0:T(8,128)} custom-call(bf16[6144,512]{1,0:T(8,128)(2,1)} %temps.1, f32[48,128]{1,0:T(8,128)} %bitcast.2, s32[48,128]{1,0:T(8,128)} %bitcast.3, s32[1]{0:T(128)S(6)} %copy.6.count), custom_call_target="tpu_custom_call" | custom-call | flops 12884901888 | bytes 6291456 | tf_op jit(solution)/shard_map/lagged_band/pallas_call | solution.py:406
  140.5 2.3 %copy.7 = f32[512,512]{1,0:T(8,128)} copy(f32[512,512]{1,0:T(8,128)} %lagged_band.1) | data formatting | bytes 2097152

commit v4 on v3

--- a/solution.py
+++ b/solution.py
@@ -12,9 +12,10 @@
 NX = 4
 NG = 8
 LANES = 128
-CHUNK = 256
+CHUNK = 128
 EARLY = 2
-WINDOW = 3
+WINDOW = 6
+BANDS = 3
 MESH = pl.DeviceIdType.MESH
 F32 = jnp.float32
 BF16 = jnp.bfloat16
@@ -23,22 +24,72 @@
 PARTS = 2
 
 
-def without(x, with_far):
-    far = (x + 2) % NX
-    pairs = [(i, k) for k in range(LAGS) for i in range(NX) if i + k < NX]
-    return [(i, k) for i, k in pairs if (far in (i, i + k)) == with_far]
-
-
-EARLY_PAIRS = list(zip(*[without(x, False) for x in range(NX)]))
-LATE_PAIRS = list(zip(*[without(x, True) for x in range(NX)]))
-CROSS_PAIRS = [[(1, 3), (2, 2), (3, 1)], [(2, 3), (3, 2)], [(3, 3)]]
+NEAR_PAIRS = list(zip(
+    [(1, 0), (3, 0), (1, 2), (0, 0), (0, 1), (0, 3)],
+    [(0, 0), (2, 0), (0, 1), (0, 2), (1, 0), (1, 1)],
+    [(1, 0), (3, 0), (1, 1), (1, 2), (2, 0), (2, 1)],
+    [(0, 0), (2, 0), (0, 2), (2, 1), (0, 3), (3, 0)],
+))
+NEXT_PAIRS = list(zip(
+    [(3, 1), (1, 3)],
+    [(2, 2), (1, 3)],
+    [(3, 2), (2, 3)],
+    [(2, 2), (3, 1)],
+))
+FAR_PAIRS = list(zip(
+    [(2, 0), (2, 1), (1, 1), (0, 2)],
+    [(3, 0), (2, 1), (0, 3), (1, 2)],
+    [(0, 0), (0, 1), (0, 2), (0, 3)],
+    [(1, 0), (1, 1), (0, 1), (1, 2)],
+))
+THEN_PAIRS = list(zip(
+    [(2, 2), (3, 2), (2, 3)],
+    [(3, 1), (2, 3), (3, 2)],
+    [(1, 3), (3, 1), (2, 2)],
+    [(1, 3), (2, 3), (3, 2)],
+))
+LAST_PAIR = (3, 3)
+OUT_AT = (5, 12, 15)
+
+
+def crossing_first(pairs, zh):
+    return sorted(pairs, key=lambda pair: pair[1] // 2 == zh)
+
+
+def out_order(zh, x):
+    def best(pool, taken):
+        def rank(pair):
+            i, k = pair
+            since = [n for n, (owner, _) in enumerate(taken) if owner == i]
+            return (i == x, k // 2 == zh, since[-1] if since else -1, pool.index(pair))
+
+        return min(pool, key=rank)
+
+    pool = [pairs[x] for pairs in NEAR_PAIRS + NEXT_PAIRS]
+    taken = []
+    for upto, more in zip(OUT_AT, (FAR_PAIRS, THEN_PAIRS, [])):
+        while len(taken) < upto:
+            pair = best(pool, taken)
+            pool.remove(pair)
+            taken.append(pair)
+        pool += [pairs[x] for pairs in more]
+    return taken
+
+
+def by_place(order):
+    return list(zip(*[order(zh, x) for zh in range(2) for x in range(NX)]))
+
+
+OUT_PAIRS = by_place(out_order)
+FAR_ORDER = by_place(lambda zh, x: crossing_first([pairs[x] for pairs in FAR_PAIRS], zh))
+THEN_ORDER = by_place(lambda zh, x: crossing_first([pairs[x] for pairs in THEN_PAIRS], zh))
 
 
 def kernel(
     temps, area, listed, count, out,
-    raw, halo, weighted, own, csend, crecv, xsend, xrecv, zsend, zrecv,
+    raw, weighted, own, csend, crecv, xsend, xrecv, between, zsend, zrecv,
     sums, near, partial, far, scale, means, scales, local_sem,
-    xs_sem, xr_sem, hs_sem, hr_sem, cs_sem, cr_sem, ps_sem, pr_sem, zs_sem, zr_sem,
+    xs_sem, xr_sem, hs_sem, hr_sem, ls_sem, lr_sem, cs_sem, cr_sem, ps_sem, pr_sem, bs_sem, zs_sem, zr_sem,
     ns_sem, nr_sem, fs_sem, fr_sem,
 ):
     row, tm = lax.axis_index("row"), lax.axis_index("tm")
@@ -103,14 +154,25 @@
 
     def forward(block, piece):
         return remote(
-            raw.at[block, rows_of(piece)], halo.at[block, rows_of(piece)],
+            raw.at[block, rows_of(piece)], weighted.at[NX + block, rows_of(piece)],
             hs_sem.at[block, piece], hr_sem.at[block, piece], g_peer(NG - 1),
         )
 
     def forward_own(piece):
         return remote(
-            temps.at[rows_of(piece, x * quarter)], halo.at[x, rows_of(piece)],
+            temps.at[rows_of(piece, x * quarter)], weighted.at[NX + x, rows_of(piece)],
             hs_sem.at[x, piece], hr_sem.at[x, piece], g_peer(NG - 1),
+        )
+
+    band = quarter // BANDS
+
+    def forward_last(part, at, mine=False):
+        r, cols = pl.ds(at * band, band), pl.ds(part * half, half)
+        source = raw.at[2, r, cols]
+        if mine:
+            source = temps.at[pl.ds(pl.multiple_of(x * quarter + at * band, band), band), cols]
+        return remote(
+            source, weighted.at[NX + 2, r, cols], ls_sem.at[part, at], lr_sem.at[part, at], g_peer(NG - 1)
         )
 
     pl.semaphore_wait(barrier, len(everyone))
@@ -119,9 +181,45 @@
         exchange(1, piece).start()
         exchange(3, piece).start()
     for piece in range(chunks):
-        @pl.when((x == 0) | ((x < NX - 1) & (piece < EARLY)))
+        @pl.when((x == 0) | ((x == 1) & (piece < EARLY)))
         def _():
             forward_own(piece).start()
+
+    @pl.when(x == 2)
+    def _():
+        forward_last(0, 0, True).start()
+
+    def send_near(step):
+        return remote(
+            sums.at[x_at[step]], near.at[NX - step - 1], ns_sem.at[step - 1], nr_sem.at[NX - step - 1], x_peer(step)
+        )
+
+    def send_far(step):
+        return remote(partial, far.at[NG - step - 1], fs_sem.at[step - 1], fr_sem.at[NG - step - 1], g_peer(step))
+
+    def one_hop(piece):
+        arrival(3, piece).wait_recv()
+        arrival(1, piece).wait_recv()
+
+        @pl.when((x == 1) | (x == 2))
+        def _():
+            forward(x - 1, piece).start()
+
+        @pl.when(x == 3)
+        def _():
+            forward(0, piece).start()
+
+        if (piece + 1) * CHUNK == band:
+            @pl.when(x == 3)
+            def _():
+                forward_last(0, 0).start()
+        if piece + WINDOW < chunks:
+            exchange(1, piece + WINDOW).start()
+            exchange(3, piece + WINDOW).start()
+        else:
+            some = chunks // WINDOW
+            for late in range(some):
+                exchange(2, (piece + WINDOW - chunks) * some + late).start()
 
     sums[...] = jnp.zeros_like(sums)
     ones = jnp.ones((8, hours), BF16)
@@ -133,44 +231,11 @@
             )
             for part in range(4):
                 sums[q, pl.ds(piece * 4 + part, 1)] = some[0:1, part * LANES : (part + 1) * LANES]
+        if q:
+            one_hop(q - 1)
     keep.wait()
-
-    def send_near(step):
-        return remote(
-            sums.at[x_at[step]], near.at[NX - step - 1], ns_sem.at[step - 1], nr_sem.at[NX - step - 1], x_peer(step)
-        )
-
-    def send_far(step):
-        return remote(partial, far.at[NG - step - 1], fs_sem.at[step - 1], fr_sem.at[NG - step - 1], g_peer(step))
-
     for step in range(1, NX):
         send_near(step).start()
-
-    def one_hop(piece):
-        arrival(3, piece).wait_recv()
-        arrival(1, piece).wait_recv()
-
-        @pl.when((x == 1) | (x == 2))
-        def _():
-            forward(x - 1, piece).start()
-
-        @pl.when(x == 3)
-        def _():
-            forward(0, piece).start()
-
-        if piece < EARLY:
-            @pl.when(x == 3)
-            def _():
-                forward(2, piece).start()
-        if piece + WINDOW < chunks:
-            exchange(1, piece + WINDOW).start()
-            exchange(3, piece + WINDOW).start()
-        else:
-            some = chunks // WINDOW
-            for late in range(some):
-                exchange(2, (piece + WINDOW - chunks) * some + late).start()
-
-    one_hop(0)
 
     live = count[0]
     groups = listed.shape[0]
@@ -185,23 +250,24 @@
         right = jnp.where(hit, 1.0, 0.0).astype(BF16)
         return mask + lax.dot_general(left, right, CROSS_LANES, preferred_element_type=F32)
 
-    mask = lax.fori_loop(0, groups, mark, jnp.zeros((groups, LANES), F32))
+    mask = jnp.zeros((groups, LANES), F32)
+    for q in range(4):
+        mask = lax.fori_loop(q * (groups // 4), (q + 1) * (groups // 4), mark, mask)
+        one_hop(3 + q)
     scale[...] = mask * area[...]
 
     def spread(row_of, target):
         for a in range(tiles):
             target[pl.ds(a * LANES, LANES)] = jnp.broadcast_to(row_of(a), (LANES, LANES)).T
 
-    spread(lambda a: scale[pl.ds(x * tiles + a, 1)], scales)
-
-    one_hop(1)
     for step in range(1, NX):
         send_near(step).wait_recv()
     partial[...] = sums[x] + near[0] + near[1] + near[2]
     for step in range(1, NG):
         send_far(step).start()
-
-    for piece in range(2, chunks):
+    one_hop(7)
+    spread(lambda a: scale[pl.ds(x * tiles + a, 1)], scales)
+    for piece in range(8, chunks):
         one_hop(piece)
 
     for piece in range(chunks):
@@ -221,17 +287,18 @@
     mean = total[:tiles] / (hours * NX * NG)
     spread(lambda a: mean[a : a + 1], means)
 
-    def weigh(source, target, piece):
+    def weigh(source, target, piece, first=0, size=None):
         r = rows_of(piece)
         m, s = means[r], scales[r]
-        for lane in range(0, hours, LANES):
+        for lane in range(first, first + (size or hours), LANES):
             at = pl.ds(lane, LANES)
             target[r, at] = ((source[r, at].astype(F32) - m) * s).astype(BF16)
 
     def pick(values):
+        at = x if len(values) == NX else zh * NX + x
         value = values[0]
-        for at in range(1, NX):
-            value = jnp.where(x == at, values[at], value)
+        for n in range(1, len(values)):
+            value = jnp.where(at == n, values[n], value)
         return value
 
     def lag_pair(pairs):
@@ -258,10 +325,10 @@
             ps_sem.at[slot, part], pr_sem.at[at, k // 2, part], (row, group * NX + i),
         )
 
-    def multiply(i, k):
+    def multiply(i, k, parts=range(PARTS)):
         slot = slot_of(i, k)
         mine = core == lax.rem(k, 2)
-        for part in range(PARTS):
+        for part in parts:
             value = lax.dot_general(
                 weighted[i + k, :, part * half : (part + 1) * half], weighted[i],
                 CROSS_ROWS, preferred_element_type=F32,
@@ -276,75 +343,143 @@
                 csend[slot, part_of(part)] = value
                 swap(slot, part).start()
 
+    def relay(i, k, part):
+        slot = slot_of(i, k)
+        return remote(
+            xsend.at[slot, part_of(part)], between.at[part, k // 2],
+            ps_sem.at[slot, part], bs_sem.at[part, k // 2], x_peer(1 if part == 0 else NX - 1),
+        )
+
+    def both_cores(slot, part):
+        at = part_of(part)
+        return own[slot, at] + crecv[slot, at]
+
     def finish(i, k):
         slot = slot_of(i, k)
+        away = lax.rem(i - x + NX, NX)
 
         @pl.when(core == lax.rem(k, 2))
         def _():
             for part in range(PARTS):
                 at = part_of(part)
                 swap(slot, part).wait_recv()
-
-                @pl.when(x == i)
-                def _():
-                    own[slot, at] = own[slot, at] + crecv[slot, at]
-
-                @pl.when(x != i)
-                def _():
-                    xsend[slot, at] = (own[slot, at] + crecv[slot, at]).astype(BF16)
+                straight = 3 if part == 0 else 1
+
+                @pl.when((away == straight) | (away == 2))
+                def _():
+                    xsend[slot, at] = both_cores(slot, part).astype(BF16)
+
+                @pl.when(away == straight)
+                def _():
                     to_owner(i, k, part).start()
+
+                @pl.when(away == 2)
+                def _():
+                    relay(i, k, part).start()
+
+                @pl.when((away == 0) | (away == NX - straight))
+                def _():
+                    own[slot, at] = both_cores(slot, part)
+
+    def pass_sum(part, kk):
+        i = x_at[1 if part == 0 else NX - 1]
+        k = kk * 2 + core
+        slot = slot_of(i, k)
+        at = part_of(part)
+
+        @pl.when((i != LAST_PAIR[0]) | (k != LAST_PAIR[1]))
+        def _():
+            relay(i, k, part).wait_recv()
+            xsend[slot, at] = (own[slot, at] + between[part, kk].astype(F32)).astype(BF16)
+            to_owner(i, k, part).start()
+
+    def finish_last(part):
+        i, k = LAST_PAIR
+        slot = slot_of(i, k)
+        at = part_of(part)
+
+        @pl.when(core == k % 2)
+        def _():
+            swap(slot, part).wait_recv()
+
+            @pl.when(x == i)
+            def _():
+                own[slot, at] = both_cores(slot, part)
+
+            @pl.when(x != i)
+            def _():
+                xsend[slot, at] = both_cores(slot, part).astype(BF16)
+                to_owner(i, k, part).start()
 
     for piece in range(chunks):
         for step in (0, 1, 3):
             weigh(raw.at[x_at[step]], weighted.at[x_at[step]], piece)
-    early = [lag_pair(pairs) for pairs in EARLY_PAIRS]
+    def take_halo(block, piece):
+        forward(block, piece).wait_recv()
+        weigh(weighted.at[NX + block], weighted.at[NX + block], piece)
+
+    ahead = jnp.where(x == 2, 1, 0)
+    near_pairs = [lag_pair(pairs) for pairs in NEAR_PAIRS]
+    next_pairs = [lag_pair(pairs) for pairs in NEXT_PAIRS]
     for piece in range(chunks):
         arrival(2, piece).wait_recv()
 
-        @pl.when(x != 1)
+        @pl.when((x == 2) | (x == 3))
         def _():
             forward(x_at[2], piece).start()
         weigh(raw.at[x_at[2]], weighted.at[x_at[2]], piece)
-        if piece < len(early):
-            multiply(*early[piece])
-    for piece in range(chunks):
-        @pl.when(x == 1)
-        def _():
-            forward(2, piece).start()
-        if piece >= EARLY:
-            @pl.when(x == 2)
-            def _():
-                forward_own(piece).start()
-
-            @pl.when(x == 3)
-            def _():
-                forward(2, piece).start()
-
-    waiting = early
-    stages = [[lag_pair(pairs) for pairs in LATE_PAIRS]] + CROSS_PAIRS
-    for stage_at, pairs in enumerate(stages):
-        if stage_at:
-            block = stage_at - 1
+        if piece < len(near_pairs):
+            multiply(*near_pairs[piece])
+        elif piece < chunks - 2:
+            for more in range(3):
+                take_halo(ahead, (piece - len(near_pairs)) * 3 + more)
+        else:
+            multiply(*next_pairs[piece - chunks + 2])
+    for part in range(PARTS):
+        for at in range(BANDS):
+            if part or at:
+                @pl.when(x == 2)
+                def _():
+                    forward_last(part, at, True).start()
+
+                @pl.when(x != 2)
+                def _():
+                    forward_last(part, at).start()
+            else:
+                @pl.when(x < 2)
+                def _():
+                    forward_last(part, at).start()
+
+    out_pairs = [lag_pair(pairs) for pairs in OUT_PAIRS]
+    sent = 0
+    for upto, pairs in zip(OUT_AT, (FAR_ORDER, THEN_ORDER, [])):
+        for pair in out_pairs[sent:upto]:
+            finish(*pair)
+        sent = upto
+        if pairs is THEN_ORDER:
             for piece in range(chunks):
-                forward(block, piece).wait_recv()
-                weigh(halo.at[block], weighted.at[NX + block], piece)
-        for pair in pairs:
-            multiply(*pair)
-            waiting.append(pair)
-            while len(waiting) > 2:
-                finish(*waiting.pop(0))
-        if stage_at < len(stages) - 1:
-            while waiting:
-                finish(*waiting.pop(0))
+                take_halo(1 - ahead, piece)
+        for each in pairs:
+            multiply(*lag_pair(each))
+    for kk in (1 - zh, zh):
+        for part in range(PARTS):
+            pass_sum(part, kk)
 
     def gathered(kk, part):
-        for d in range(NX - 1):
-            remote(
+        def came(d):
+            return remote(
                 xsend.at[0, part_of(part)], xrecv.at[d, kk, part_of(part)],
                 ps_sem.at[0, part], pr_sem.at[d, kk, part], x_peer(d + 1),
-            ).wait_recv()
+            )
+
+        @pl.when((x == LAST_PAIR[0]) & (kk * 2 + core == LAST_PAIR[1]))
+        def _():
+            came(1).wait_recv()
+            slot, at = slot_of(*LAST_PAIR), part_of(part)
+            own[slot, at] = own[slot, at] + xrecv[1, LAST_PAIR[1] // 2, at].astype(F32)
         value = own[x * 2 + kk, part_of(part)]
-        for d in range(NX - 1):
+        for d in (0, 2):
+            came(d).wait_recv()
             value = value + xrecv[d, kk, part_of(part)].astype(F32)
         return value
 
@@ -359,12 +494,17 @@
             across(part).start()
 
     last = (x == NX - 1) & (core == 1) & (zh == 0)
-
-    @pl.when(jnp.logical_not(last))
-    def _():
-        send_across()
-    while waiting:
-        finish(*waiting.pop(0))
+    for part in range(PARTS):
+        for at in range(BANDS):
+            forward_last(part, at).wait_recv()
+            for piece in range(at * band // CHUNK, (at + 1) * band // CHUNK):
+                weigh(weighted.at[NX + 2], weighted.at[NX + 2], piece, part * half, half)
+        multiply(*LAST_PAIR, [part])
+        if not part:
+            @pl.when(jnp.logical_not(last))
+            def _():
+                send_across()
+        finish_last(part)
 
     @pl.when(last)
     def _():
@@ -380,9 +520,12 @@
         send_near(step).wait_send()
     for step in range(1, NG):
         send_far(step).wait_send()
-    for block in range(NX - 1):
+    for block in range(NX - 2):
         for piece in range(chunks):
             forward(block, piece).wait_send()
+    for part in range(PARTS):
+        for at in range(BANDS):
+            forward_last(part, at).wait_send()
     for i in range(NX):
         for k in range(LAGS):
             for part in range(PARTS):
@@ -412,13 +555,13 @@
         out_specs=vmem,
         scratch_shapes=[
             pltpu.VMEM((NX, quarter, hours), BF16),
-            pltpu.VMEM((NX - 1, quarter, hours), BF16),
             pltpu.VMEM((2 * NX - 1, quarter, hours), BF16),
             pltpu.VMEM((2 * NX, hours, hours), F32),
             pltpu.VMEM((2 * NX, hours, hours), F32),
             pltpu.VMEM((2 * NX, hours, hours), F32),
             pltpu.VMEM((2 * NX, hours, hours), BF16),
             pltpu.VMEM((NX - 1, 2, hours, hours), BF16),
+            pltpu.VMEM((PARTS, 2, hours // PARTS, hours), BF16),
             pltpu.VMEM((hours, hours), BF16),
             pltpu.VMEM((hours, hours), BF16),
             pltpu.VMEM((NX, 16, LANES), F32),
@@ -430,9 +573,10 @@
             pltpu.VMEM((quarter, LANES), F32),
             dma((NX + 1,)),
             dma((NX - 1, chunks)), dma((NX - 1, chunks)),
-            dma((NX - 1, chunks)), dma((NX - 1, chunks)),
+            dma((NX - 2, chunks)), dma((NX - 2, chunks)),
+            dma((PARTS, BANDS)), dma((PARTS, BANDS)),
             dma((2 * NX, PARTS)), dma((2 * NX, PARTS)),
-            dma((2 * NX, PARTS)), dma((NX - 1, 2, PARTS)),
+            dma((2 * NX, PARTS)), dma((NX - 1, 2, PARTS)), dma((PARTS, 2)),
             dma((PARTS,)), dma((PARTS,)),
             dma((NX - 1,)), dma((NX - 1,)),
             dma((NG - 1,)), dma((NG - 1,)),

time: 143 us -> 136 us (0.951)
  Pallas kernels: 140 us -> 132 us
    pallas_call x1, Pallas kernels: 140 us -> 132 us  [body(): pl.pallas_call(kernel, out_shape=jax.ShapeDtypeStruct((hours, hours), F32...]
where the time goes in v4:
time: 136 us; the launch traced here: 135 us
  Pallas kernels  132 us (97%)
  local copies, waits for them, and re-layouts  2.26 us (2%)
    pallas_call x1, Pallas kernels, body(): pl.pallas_call(kernel, out_shape=jax.ShapeDtypeStruct((hours, hours), F32...  132 us

profile of v4, /device:TPU:71, one launch (start us, length us, event | category | flops | bytes accessed | tf_op | source)
XLA Modules:
  0.0 135.3 jit_solution(10375692693364883103)
XLA Ops:
  0.7 132.4 %lagged_band.1 = f32[512,512]{1,0:T(8,128)} custom-call(bf16[6144,512]{1,0:T(8,128)(2,1)} %temps.1, f32[48,128]{1,0:T(8,128)} %bitcast.2, s32[48,128]{1,0:T(8,128)} %bitcast.3, s32[1]{0:T(128)S(6)} %copy.6.count), custom_call_target="tpu_custom_call" | custom-call | flops 12884901888 | bytes 6291456 | tf_op jit(solution)/shard_map/lagged_band/pallas_call | solution.py:549
  133.1 2.3 %copy.7 = f32[512,512]{1,0:T(8,128)} copy(f32[512,512]{1,0:T(8,128)} %lagged_band.1) | data formatting | bytes 2097152

commit v5 on v4

--- a/solution.py
+++ b/solution.py
@@ -16,6 +16,7 @@
 EARLY = 2
 WINDOW = 6
 BANDS = 3
+LAST_PARTS = 4
 MESH = pl.DeviceIdType.MESH
 F32 = jnp.float32
 BF16 = jnp.bfloat16
@@ -91,6 +92,7 @@
     sums, near, partial, far, scale, means, scales, local_sem,
     xs_sem, xr_sem, hs_sem, hr_sem, ls_sem, lr_sem, cs_sem, cr_sem, ps_sem, pr_sem, bs_sem, zs_sem, zr_sem,
     ns_sem, nr_sem, fs_sem, fr_sem,
+    lcs_sem, lcr_sem, lps_sem, lpr_sem, lzs_sem, lzr_sem,
 ):
     row, tm = lax.axis_index("row"), lax.axis_index("tm")
     zh, core = row // 2, lax.rem(row, 2)
@@ -165,9 +167,13 @@
         )
 
     band = quarter // BANDS
+    thin = hours // LAST_PARTS
+
+    def last_part(part):
+        return pl.ds(part * thin, thin)
 
     def forward_last(part, at, mine=False):
-        r, cols = pl.ds(at * band, band), pl.ds(part * half, half)
+        r, cols = pl.ds(at * band, band), last_part(part)
         source = raw.at[2, r, cols]
         if mine:
             source = temps.at[pl.ds(pl.multiple_of(x * quarter + at * band, band), band), cols]
@@ -231,8 +237,8 @@
             )
             for part in range(4):
                 sums[q, pl.ds(piece * 4 + part, 1)] = some[0:1, part * LANES : (part + 1) * LANES]
-        if q:
-            one_hop(q - 1)
+        if q < 3:
+            one_hop(q)
     keep.wait()
     for step in range(1, NX):
         send_near(step).start()
@@ -325,10 +331,10 @@
             ps_sem.at[slot, part], pr_sem.at[at, k // 2, part], (row, group * NX + i),
         )
 
-    def multiply(i, k, parts=range(PARTS)):
+    def multiply(i, k):
         slot = slot_of(i, k)
         mine = core == lax.rem(k, 2)
-        for part in parts:
+        for part in range(PARTS):
             value = lax.dot_general(
                 weighted[i + k, :, part * half : (part + 1) * half], weighted[i],
                 CROSS_ROWS, preferred_element_type=F32,
@@ -393,23 +399,69 @@
             xsend[slot, at] = (own[slot, at] + between[part, kk].astype(F32)).astype(BF16)
             to_owner(i, k, part).start()
 
+    last_slot, last_kk = slot_of(*LAST_PAIR), LAST_PAIR[1] // 2
+    last_mine = core == LAST_PAIR[1] % 2
+
+    def swap_last(part):
+        at = last_part(part)
+        return remote(csend.at[last_slot, at], crecv.at[last_slot, at], lcs_sem.at[part], lcr_sem.at[part], partner)
+
+    def last_to_owner(part):
+        away = lax.rem(x - LAST_PAIR[0] + NX, NX)
+        place = lax.rem(away + NX - 1, NX)
+        at = last_part(part)
+        return remote(
+            xsend.at[last_slot, at], xrecv.at[place, last_kk, at],
+            lps_sem.at[part], lpr_sem.at[place, part], (row, group * NX + LAST_PAIR[0]),
+        )
+
+    def multiply_last(part):
+        i, k = LAST_PAIR
+        at = last_part(part)
+        value = lax.dot_general(
+            weighted[i + k, :, part * thin : (part + 1) * thin], weighted[i],
+            CROSS_ROWS, preferred_element_type=F32,
+        )
+
+        @pl.when(last_mine)
+        def _():
+            own[last_slot, at] = value
+
+        @pl.when(jnp.logical_not(last_mine))
+        def _():
+            csend[last_slot, at] = value
+            swap_last(part).start()
+
     def finish_last(part):
-        i, k = LAST_PAIR
-        slot = slot_of(i, k)
-        at = part_of(part)
-
-        @pl.when(core == k % 2)
-        def _():
-            swap(slot, part).wait_recv()
-
-            @pl.when(x == i)
+        at = last_part(part)
+
+        @pl.when(last_mine)
+        def _():
+            swap_last(part).wait_recv()
+            value = own[last_slot, at] + crecv[last_slot, at]
+
+            @pl.when(x == LAST_PAIR[0])
             def _():
-                own[slot, at] = both_cores(slot, part)
-
-            @pl.when(x != i)
+                own[last_slot, at] = value
+
+            @pl.when(x != LAST_PAIR[0])
             def _():
-                xsend[slot, at] = both_cores(slot, part).astype(BF16)
-                to_owner(i, k, part).start()
+                xsend[last_slot, at] = value.astype(BF16)
+                last_to_owner(part).start()
+
+    def gathered_last(part):
+        at = last_part(part)
+        value = own[last_slot, at]
+        for d in range(NX - 1):
+            remote(
+                xsend.at[last_slot, at], xrecv.at[d, last_kk, at], lps_sem.at[part], lpr_sem.at[d, part], x_peer(d + 1)
+            ).wait_recv()
+            value = value + xrecv[d, last_kk, at].astype(F32)
+        return value
+
+    def across_last(part):
+        at = last_part(part)
+        return remote(zsend.at[at], zrecv.at[at], lzs_sem.at[part], lzr_sem.at[part], opposite)
 
     for piece in range(chunks):
         for step in (0, 1, 3):
@@ -435,7 +487,7 @@
                 take_halo(ahead, (piece - len(near_pairs)) * 3 + more)
         else:
             multiply(*next_pairs[piece - chunks + 2])
-    for part in range(PARTS):
+    for part in range(LAST_PARTS):
         for at in range(BANDS):
             if part or at:
                 @pl.when(x == 2)
@@ -472,11 +524,6 @@
                 ps_sem.at[0, part], pr_sem.at[d, kk, part], x_peer(d + 1),
             )
 
-        @pl.when((x == LAST_PAIR[0]) & (kk * 2 + core == LAST_PAIR[1]))
-        def _():
-            came(1).wait_recv()
-            slot, at = slot_of(*LAST_PAIR), part_of(part)
-            own[slot, at] = own[slot, at] + xrecv[1, LAST_PAIR[1] // 2, at].astype(F32)
         value = own[x * 2 + kk, part_of(part)]
         for d in (0, 2):
             came(d).wait_recv()
@@ -493,26 +540,45 @@
             zsend[part_of(part)] = gathered(1 - zh, part).astype(BF16)
             across(part).start()
 
-    last = (x == NX - 1) & (core == 1) & (zh == 0)
-    for part in range(PARTS):
+    owner = (x == LAST_PAIR[0]) & last_mine & (zh == last_kk)
+    sender = (x == LAST_PAIR[0]) & last_mine & (zh != last_kk)
+    for part in range(LAST_PARTS):
         for at in range(BANDS):
             forward_last(part, at).wait_recv()
             for piece in range(at * band // CHUNK, (at + 1) * band // CHUNK):
-                weigh(weighted.at[NX + 2], weighted.at[NX + 2], piece, part * half, half)
-        multiply(*LAST_PAIR, [part])
-        if not part:
-            @pl.when(jnp.logical_not(last))
+                weigh(weighted.at[NX + 2], weighted.at[NX + 2], piece, part * thin, thin)
+        multiply_last(part)
+        if part == 1:
+            @pl.when(jnp.logical_not(sender))
             def _():
                 send_across()
-        finish_last(part)
-
-    @pl.when(last)
+        if part:
+            finish_last(part - 1)
+    finish_last(LAST_PARTS - 1)
+
+    @pl.when(sender)
     def _():
-        send_across()
-    for part in range(PARTS):
-        value = gathered(zh, part)
-        across(part).wait_recv()
-        out[part_of(part)] = (value + zrecv[part_of(part)].astype(F32)) / math.sqrt(quarter * NX * 4)
+        for part in range(LAST_PARTS):
+            zsend[last_part(part)] = gathered_last(part).astype(BF16)
+            across_last(part).start()
+
+    divisor = math.sqrt(quarter * NX * 4)
+
+    @pl.when(owner)
+    def _():
+        for part in range(LAST_PARTS):
+            at = last_part(part)
+            value = gathered_last(part)
+            across_last(part).wait_recv()
+            out[at] = (value + zrecv[at].astype(F32)) / divisor
+
+    @pl.when(jnp.logical_not(owner))
+    def _():
+        for part in range(PARTS):
+            at = part_of(part)
+            value = gathered(zh, part)
+            across(part).wait_recv()
+            out[at] = (value + zrecv[at].astype(F32)) / divisor
 
     for step in range(1, NX):
         for piece in range(chunks):
@@ -523,11 +589,13 @@
     for block in range(NX - 2):
         for piece in range(chunks):
             forward(block, piece).wait_send()
-    for part in range(PARTS):
+    for part in range(LAST_PARTS):
         for at in range(BANDS):
             forward_last(part, at).wait_send()
     for i in range(NX):
         for k in range(LAGS):
+            if (i, k) == LAST_PAIR:
+                continue
             for part in range(PARTS):
                 @pl.when(core != k % 2)
                 def _():
@@ -536,8 +604,22 @@
                 @pl.when((core == k % 2) & (x != i))
                 def _():
                     to_owner(i, k, part).wait_send()
+    for part in range(LAST_PARTS):
+        @pl.when(jnp.logical_not(last_mine))
+        def _():
+            swap_last(part).wait_send()
+
+        @pl.when(last_mine & (x != LAST_PAIR[0]))
+        def _():
+            last_to_owner(part).wait_send()
+
+        @pl.when(sender)
+        def _():
+            across_last(part).wait_send()
     for part in range(PARTS):
-        across(part).wait_send()
+        @pl.when(jnp.logical_not(sender))
+        def _():
+            across(part).wait_send()
 
 
 def body(temps, area, ocean_rows, counts):
@@ -548,7 +630,7 @@
     dma = pltpu.SemaphoreType.DMA
     return pl.pallas_call(
         kernel,
-        out_shape=jax.ShapeDtypeStruct((hours, hours), F32),
+        out_shape=pltpu.VMEM((hours, hours), F32),
         in_specs=[
             pl.BlockSpec(memory_space=pl.ANY), vmem, vmem, pl.BlockSpec(memory_space=pltpu.SMEM),
         ],
@@ -574,15 +656,18 @@
             dma((NX + 1,)),
             dma((NX - 1, chunks)), dma((NX - 1, chunks)),
             dma((NX - 2, chunks)), dma((NX - 2, chunks)),
-            dma((PARTS, BANDS)), dma((PARTS, BANDS)),
+            dma((LAST_PARTS, BANDS)), dma((LAST_PARTS, BANDS)),
             dma((2 * NX, PARTS)), dma((2 * NX, PARTS)),
             dma((2 * NX, PARTS)), dma((NX - 1, 2, PARTS)), dma((PARTS, 2)),
             dma((PARTS,)), dma((PARTS,)),
             dma((NX - 1,)), dma((NX - 1,)),
             dma((NG - 1,)), dma((NG - 1,)),
+            dma((LAST_PARTS,)), dma((LAST_PARTS,)),
+            dma((LAST_PARTS,)), dma((NX - 1, LAST_PARTS)),
+            dma((LAST_PARTS,)), dma((LAST_PARTS,)),
         ],
         compiler_params=pltpu.CompilerParams(
-            collective_id=0, has_side_effects=True, vmem_limit_bytes=62 << 20
+            collective_id=0, has_side_effects=True, vmem_limit_bytes=56 << 20
         ),
         cost_estimate=pl.CostEstimate(
             flops=2 * LAGS * hours * hours * rows, bytes_accessed=2 * rows * hours, transcendentals=0

time: 136 us -> 133 us (0.978)
  Pallas kernels: 132 us -> 130 us
    pallas_call x1, Pallas kernels: 132 us -> 130 us  [body(): pl.pallas_call(kernel, out_shape=pltpu.VMEM((hours, hours), F32), in_spec...]
where the time goes in v5:
time: 133 us; the launch traced here: 132 us
  Pallas kernels  130 us (98%)
    pallas_call x1, Pallas kernels, body(): pl.pallas_call(kernel, out_shape=pltpu.VMEM((hours, hours), F32), in_spec...  130 us

profile of v5, /device:TPU:71, one launch (start us, length us, event | category | flops | bytes accessed | tf_op | source)
XLA Modules:
  0.0 132.1 jit_solution(10913516872868501959)
XLA Ops:
  0.7 130.5 %lagged_band.1 = f32[512,512]{1,0:T(8,128)S(1)} custom-call(bf16[6144,512]{1,0:T(8,128)(2,1)} %temps.1, f32[48,128]{1,0:T(8,128)} %bitcast.2, s32[48,128]{1,0:T(8,128)} %bitcast.3, s32[1]{0:T(128)S(6)} %copy.7.count), custom_call_target="tpu_custom_call" | custom-call | flops 12884901888 | bytes 6291456 | tf_op jit(solution)/shard_map/lagged_band/pallas_call | solution.py:631
  131.1 1.0 copy.6

commit v6 on v5

--- a/solution.py
+++ b/solution.py
@@ -16,6 +16,7 @@
 EARLY = 2
 WINDOW = 6
 BANDS = 3
+AHEAD = ((0, 0), (1, 0), (0, 1))
 LAST_PARTS = 4
 MESH = pl.DeviceIdType.MESH
 F32 = jnp.float32
@@ -87,9 +88,9 @@
 
 
 def kernel(
-    temps, area, listed, count, out,
+    temps, area_in, listed_in, count, out,
     raw, weighted, own, csend, crecv, xsend, xrecv, between, zsend, zrecv,
-    sums, near, partial, far, scale, means, scales, local_sem,
+    sums, near, partial, far, area, listed, scale, means, scales, local_sem,
     xs_sem, xr_sem, hs_sem, hr_sem, ls_sem, lr_sem, cs_sem, cr_sem, ps_sem, pr_sem, bs_sem, zs_sem, zr_sem,
     ns_sem, nr_sem, fs_sem, fr_sem,
     lcs_sem, lcr_sem, lps_sem, lpr_sem, lzs_sem, lzr_sem,
@@ -139,6 +140,12 @@
     for copy in stage:
         copy.start()
     keep.start()
+    tables = [
+        pltpu.make_async_copy(area_in, area, local_sem.at[NX + 1]),
+        pltpu.make_async_copy(listed_in, listed, local_sem.at[NX + 2]),
+    ]
+    for copy in tables:
+        copy.start()
 
     def exchange(step, piece):
         target = x_at[step]
@@ -184,16 +191,21 @@
     pl.semaphore_wait(barrier, len(everyone))
 
     for piece in range(WINDOW):
+        exchange(3, piece).start()
         exchange(1, piece).start()
-        exchange(3, piece).start()
-    for piece in range(chunks):
-        @pl.when((x == 0) | ((x == 1) & (piece < EARLY)))
+        if piece < EARLY:
+            @pl.when(x < 2)
+            def _():
+                forward_own(piece).start()
+    for piece in range(EARLY, chunks):
+        @pl.when(x == 0)
         def _():
             forward_own(piece).start()
 
     @pl.when(x == 2)
     def _():
-        forward_last(0, 0, True).start()
+        for part, at in AHEAD:
+            forward_last(part, at, True).start()
 
     def send_near(step):
         return remote(
@@ -215,10 +227,11 @@
         def _():
             forward(0, piece).start()
 
-        if (piece + 1) * CHUNK == band:
-            @pl.when(x == 3)
-            def _():
-                forward_last(0, 0).start()
+        for part, at in AHEAD:
+            if (piece + 1) * CHUNK == (at + 1) * band:
+                @pl.when(x == 3)
+                def _():
+                    forward_last(part, at).start()
         if piece + WINDOW < chunks:
             exchange(1, piece + WINDOW).start()
             exchange(3, piece + WINDOW).start()
@@ -226,6 +239,9 @@
             some = chunks // WINDOW
             for late in range(some):
                 exchange(2, (piece + WINDOW - chunks) * some + late).start()
+
+    one_hop(0)
+    one_hop(1)
 
     sums[...] = jnp.zeros_like(sums)
     ones = jnp.ones((8, hours), BF16)
@@ -238,8 +254,10 @@
             for part in range(4):
                 sums[q, pl.ds(piece * 4 + part, 1)] = some[0:1, part * LANES : (part + 1) * LANES]
         if q < 3:
-            one_hop(q)
+            one_hop(q + 2)
     keep.wait()
+    for copy in tables:
+        copy.wait()
     for step in range(1, NX):
         send_near(step).start()
 
@@ -259,7 +277,7 @@
     mask = jnp.zeros((groups, LANES), F32)
     for q in range(4):
         mask = lax.fori_loop(q * (groups // 4), (q + 1) * (groups // 4), mark, mask)
-        one_hop(3 + q)
+        one_hop(5 + q)
     scale[...] = mask * area[...]
 
     def spread(row_of, target):
@@ -271,9 +289,9 @@
     partial[...] = sums[x] + near[0] + near[1] + near[2]
     for step in range(1, NG):
         send_far(step).start()
-    one_hop(7)
+    one_hop(9)
     spread(lambda a: scale[pl.ds(x * tiles + a, 1)], scales)
-    for piece in range(8, chunks):
+    for piece in range(10, chunks):
         one_hop(piece)
 
     for piece in range(chunks):
@@ -284,14 +302,6 @@
             @pl.when(x == 1)
             def _():
                 forward_own(piece).start()
-
-    for step in range(1, NG):
-        send_far(step).wait_recv()
-    total = partial[...]
-    for step in range(NG - 1):
-        total = total + far[step]
-    mean = total[:tiles] / (hours * NX * NG)
-    spread(lambda a: mean[a : a + 1], means)
 
     def weigh(source, target, piece, first=0, size=None):
         r = rows_of(piece)
@@ -463,9 +473,6 @@
         at = last_part(part)
         return remote(zsend.at[at], zrecv.at[at], lzs_sem.at[part], lzr_sem.at[part], opposite)
 
-    for piece in range(chunks):
-        for step in (0, 1, 3):
-            weigh(raw.at[x_at[step]], weighted.at[x_at[step]], piece)
     def take_halo(block, piece):
         forward(block, piece).wait_recv()
         weigh(weighted.at[NX + block], weighted.at[NX + block], piece)
@@ -473,23 +480,37 @@
     ahead = jnp.where(x == 2, 1, 0)
     near_pairs = [lag_pair(pairs) for pairs in NEAR_PAIRS]
     next_pairs = [lag_pair(pairs) for pairs in NEXT_PAIRS]
+    def take_means():
+        for step in range(1, NG):
+            send_far(step).wait_recv()
+        total = partial[...]
+        for step in range(NG - 1):
+            total = total + far[step]
+        mean = total[:tiles] / (hours * NX * NG)
+        spread(lambda a: mean[a : a + 1], means)
+
     for piece in range(chunks):
         arrival(2, piece).wait_recv()
 
         @pl.when((x == 2) | (x == 3))
         def _():
             forward(x_at[2], piece).start()
+        if not piece:
+            take_means()
         weigh(raw.at[x_at[2]], weighted.at[x_at[2]], piece)
-        if piece < len(near_pairs):
-            multiply(*near_pairs[piece])
-        elif piece < chunks - 2:
-            for more in range(3):
-                take_halo(ahead, (piece - len(near_pairs)) * 3 + more)
+        if piece < 4:
+            for each in range(piece * 3, piece * 3 + 3):
+                for step in (0, 1, 3):
+                    weigh(raw.at[x_at[step]], weighted.at[x_at[step]], each)
+        elif piece < 10:
+            multiply(*near_pairs[piece - 4])
+            for each in range(2):
+                take_halo(ahead, (piece - 4) * 2 + each)
         else:
-            multiply(*next_pairs[piece - chunks + 2])
+            multiply(*next_pairs[piece - 10])
     for part in range(LAST_PARTS):
         for at in range(BANDS):
-            if part or at:
+            if (part, at) not in AHEAD:
                 @pl.when(x == 2)
                 def _():
                     forward_last(part, at, True).start()
@@ -627,12 +648,13 @@
     quarter = rows // NX
     chunks = quarter // CHUNK
     vmem = pl.BlockSpec(memory_space=pltpu.VMEM)
+    any_space = pl.BlockSpec(memory_space=pl.ANY)
     dma = pltpu.SemaphoreType.DMA
     return pl.pallas_call(
         kernel,
         out_shape=pltpu.VMEM((hours, hours), F32),
         in_specs=[
-            pl.BlockSpec(memory_space=pl.ANY), vmem, vmem, pl.BlockSpec(memory_space=pltpu.SMEM),
+            any_space, any_space, any_space, pl.BlockSpec(memory_space=pltpu.SMEM),
         ],
         out_specs=vmem,
         scratch_shapes=[
@@ -651,9 +673,11 @@
             pltpu.VMEM((16, LANES), F32),
             pltpu.VMEM((NG - 1, 16, LANES), F32),
             pltpu.VMEM((rows // LANES, LANES), F32),
+            pltpu.VMEM((rows // LANES, LANES), jnp.int32),
+            pltpu.VMEM((rows // LANES, LANES), F32),
             pltpu.VMEM((quarter, LANES), F32),
             pltpu.VMEM((quarter, LANES), F32),
-            dma((NX + 1,)),
+            dma((NX + 3,)),
             dma((NX - 1, chunks)), dma((NX - 1, chunks)),
             dma((NX - 2, chunks)), dma((NX - 2, chunks)),
             dma((LAST_PARTS, BANDS)), dma((LAST_PARTS, BANDS)),

time: 133 us -> 132 us (level)
  no operation moved by 1% of the time
where the time goes in v6:
time: 132 us; the launch traced here: 131 us
  Pallas kernels  130 us (98%)
    pallas_call x1, Pallas kernels, body(): pl.pallas_call(kernel, out_shape=pltpu.VMEM((hours, hours), F32), in_spec...  130 us

profile of v6, /device:TPU:71, one launch (start us, length us, event | category | flops | bytes accessed | tf_op | source)
XLA Modules:
  0.0 131.4 jit_solution(6587294668913754512)
XLA Ops:
  0.7 129.8 %lagged_band.1 = f32[512,512]{1,0:T(8,128)S(1)} custom-call(bf16[6144,512]{1,0:T(8,128)(2,1)} %temps.1, f32[48,128]{1,0:T(8,128)} %bitcast.2, s32[48,128]{1,0:T(8,128)} %bitcast.3, s32[1]{0:T(128)S(6)} %copy.7.count), custom_call_target="tpu_custom_call" | custom-call | flops 12884901888 | bytes 6291456 | tf_op jit(solution)/shard_map/lagged_band/pallas_call | solution.py:653
  130.5 1.0 copy.6

commit v7 on v6

--- a/solution.py
+++ b/solution.py
@@ -216,16 +216,20 @@
         return remote(partial, far.at[NG - step - 1], fs_sem.at[step - 1], fr_sem.at[NG - step - 1], g_peer(step))
 
     def one_hop(piece):
-        arrival(3, piece).wait_recv()
-        arrival(1, piece).wait_recv()
-
-        @pl.when((x == 1) | (x == 2))
-        def _():
-            forward(x - 1, piece).start()
-
         @pl.when(x == 3)
         def _():
+            arrival(1, piece).wait_recv()
             forward(0, piece).start()
+            arrival(3, piece).wait_recv()
+
+        @pl.when(x != 3)
+        def _():
+            arrival(3, piece).wait_recv()
+
+            @pl.when(x != 0)
+            def _():
+                forward(x - 1, piece).start()
+            arrival(1, piece).wait_recv()
 
         for part, at in AHEAD:
             if (piece + 1) * CHUNK == (at + 1) * band:

time: 132 us -> 132 us (level)
  no operation moved by 1% of the time
where the time goes in v7:
time: 132 us; the launch traced here: 131 us
  Pallas kernels  130 us (98%)
    pallas_call x1, Pallas kernels, body(): pl.pallas_call(kernel, out_shape=pltpu.VMEM((hours, hours), F32), in_spec...  130 us

profile of v7, /device:TPU:71, one launch (start us, length us, event | category | flops | bytes accessed | tf_op | source)
XLA Modules:
  0.0 131.4 jit_solution(15525908536277352942)
XLA Ops:
  0.7 129.8 %lagged_band.1 = f32[512,512]{1,0:T(8,128)S(1)} custom-call(bf16[6144,512]{1,0:T(8,128)(2,1)} %temps.1, f32[48,128]{1,0:T(8,128)} %bitcast.2, s32[48,128]{1,0:T(8,128)} %bitcast.3, s32[1]{0:T(128)S(6)} %copy.7.count), custom_call_target="tpu_custom_call" | custom-call | flops 12884901888 | bytes 6291456 | tf_op jit(solution)/shard_map/lagged_band/pallas_call | solution.py:657
  130.5 1.0 copy.6
